TPU v7x, 512 devices: a whole 4x4x16 slice. The times are simulated.
512 devices in a mesh: label: 64 (over y, z), cent: 8 (over x, core).
Axes of the slice: x: 4, y: 4, z: 16, core: 2. Of those that a mesh axis runs over, the one named last changes fastest.
Arguments:
- labels: bfloat16 [32768, 256], P('label'), may hold values from -6 to 6
- counts: int32 [64], P('label'), may hold values from 1 to 512, 16384 in all
- centroids: bfloat16 [32768, 256], P('cent'), may hold values from -6 to 6
Outputs:
- new_centroids: float32 [32768, 256], P(('cent', 'label'))
- code_mass: float32 [32768], P('cent')
Inputs may be any that keep to these rules, and one draw needn't show every extreme that they name: Label device i holds its live rows in its first counts[i] slots, the rest are padding; the counts sum to 16384 and at least one device has all 512 slots live.
All inputs are finite; a program needn't handle non-finite values.
Results may differ from a plain program's by a relative error of at most 0.0072.
Values sent between devices are 32-bit elements; how exact they have to be, the bound alone decides.
A program may use at most 64 MiB of HBM per device.

v0:
```python
import jax
import jax.numpy as jnp
from jax import lax
from jax.sharding import PartitionSpec as P

ITERS = 3


SOFTMAX_HEAT = 0.02
EPSILON = 1e-06


def unit_rows(input_values):
    widened = input_values.astype(jnp.float32)
    scale = lax.rsqrt(jnp.mean(widened * widened, axis=1, keepdims=True) + EPSILON)
    return (widened * scale).astype(jnp.bfloat16)


def column_part(row_scale, gibbs_kernel):
    return jnp.dot(
        row_scale, gibbs_kernel, preferred_element_type=jnp.float32, precision=lax.Precision.HIGHEST
    )


def column_total(local_sum, finish):
    summed = lax.psum(local_sum, "label")
    return finish(summed, 0)


def shards(labels, counts, centroids):
    label_row_count, feature_total_count = labels.shape
    label_unit = unit_rows(labels)
    centroid_unit = unit_rows(centroids)
    affinity_scores = lax.dot_general(
        label_unit, centroid_unit, (((1,), (1,)), ((), ())), preferred_element_type=jnp.float32
    )
    gibbs_kernel = jnp.exp(affinity_scores * (1.0 / (SOFTMAX_HEAT * feature_total_count))).astype(
        jnp.bfloat16
    )
    live_mask = (jnp.arange(label_row_count, dtype=jnp.int32) < counts[0]).astype(jnp.float32)
    row_scale = live_mask
    col_scale = jnp.ones((gibbs_kernel.shape[1],), jnp.float32)
    for iteration in range(ITERS):
        col_scale = column_total(
            column_part(row_scale, gibbs_kernel), lambda summed, offset: 1.0 / summed
        )
        row_local = jnp.dot(
            gibbs_kernel,
            col_scale,
            preferred_element_type=jnp.float32,
            precision=lax.Precision.HIGHEST,
        )
        row_sum = lax.psum(row_local, "cent")
        row_scale = live_mask / row_sum
    final_scale = col_scale

    def scaled_mass(summed, offset):
        return final_scale * summed

    code_mass = column_total(column_part(row_scale, gibbs_kernel), scaled_mass)
    plan_weights = (row_scale[:, None] * gibbs_kernel).astype(jnp.bfloat16)
    stats = lax.psum_scatter(
        lax.dot_general(
            plan_weights, label_unit, (((0,), (0,)), ((), ())), preferred_element_type=jnp.float32
        ),
        "label",
        scatter_dimension=0,
        tiled=True,
    )
    new_centroids = stats * lax.rsqrt(jnp.mean(stats * stats, axis=1, keepdims=True) + EPSILON)
    return (new_centroids, code_mass)


def solution(mesh):
    placed = (P("label", None), P("label"), P("cent", None))
    return jax.shard_map(
        shards,
        mesh=mesh,
        in_specs=placed,
        out_specs=(P(("cent", "label"), None), P("cent")),
        check_vma=False,
    )
```

profile of v0, /device:TPU:1, one launch (start us, length us, event | category | flops | bytes accessed | tf_op | source)
XLA Modules:
  0.0 1604.6 jit_solution(7758326635039702441)
XLA Ops:
  7.2 0.0 reduce-scatter.2.cloned.1.call-start
  7.2 1.1 fusion.6
  8.3 2.2 fusion
  11.2 3.4 exponential_convert_fusion
  14.7 1.9 copy-done
  16.6 0.6 fusion.11
  17.3 231.5 %psum.49 = f32[4096]{0:T(1024)S(1)} all-reduce(f32[4096]{0:T(1024)S(1)} %bitcast.33), channel_id=1, replica_groups=mesh['label'=64,'cent'=8] {'label'}, use_global_device_ids=true, to_apply=%region_2.0 | all-reduce | flops 4096 | bytes 32768 | tf_op jit(solution)/shard_map/psum | solution.py:26
  248.8 5.5 fusion.12
  254.3 67.6 %psum.50 = f32[512]{0:T(512)S(1)} all-reduce(f32[512]{0:T(512)S(1)} %bitcast.40), channel_id=1, replica_groups=mesh['label'=64,'cent'=8] {'cent'}, use_global_device_ids=true, to_apply=%region_3.0 | all-reduce | flops 512 | bytes 4096 | tf_op jit(solution)/shard_map/psum | solution.py:53
  321.9 3.9 fusion.13
  325.8 218.9 %psum.51 = f32[4096]{0:T(1024)S(1)} all-reduce(f32[4096]{0:T(1024)S(1)} %bitcast.35), channel_id=1, replica_groups=mesh['label'=64,'cent'=8] {'label'}, use_global_device_ids=true, to_apply=%region_4.0 | all-reduce | flops 4096 | bytes 32768 | tf_op jit(solution)/shard_map/psum | solution.py:26
  544.8 5.5 fusion.14
  550.3 67.4 %psum.52 = f32[512]{0:T(512)S(1)} all-reduce(f32[512]{0:T(512)S(1)} %bitcast.42), channel_id=1, replica_groups=mesh['label'=64,'cent'=8] {'cent'}, use_global_device_ids=true, to_apply=%region_5.0 | all-reduce | flops 512 | bytes 4096 | tf_op jit(solution)/shard_map/psum | solution.py:53
  617.7 4.0 fusion.15
  621.7 219.1 %psum.53 = f32[4096]{0:T(1024)S(1)} all-reduce(f32[4096]{0:T(1024)S(1)} %bitcast.37), channel_id=1, replica_groups=mesh['label'=64,'cent'=8] {'label'}, use_global_device_ids=true, to_apply=%region_6.0 | all-reduce | flops 4096 | bytes 32768 | tf_op jit(solution)/shard_map/psum | solution.py:26
  840.8 5.5 fusion.16
  846.4 67.4 %psum.54 = f32[512]{0:T(512)S(1)} all-reduce(f32[512]{0:T(512)S(1)} %bitcast.44), channel_id=1, replica_groups=mesh['label'=64,'cent'=8] {'cent'}, use_global_device_ids=true, to_apply=%region_7.0 | all-reduce | flops 512 | bytes 4096 | tf_op jit(solution)/shard_map/psum | solution.py:53
  913.8 6.0 fusion.2
  919.9 3.9 fusion.17
  923.8 219.1 %psum.55 = f32[4096]{0:T(1024)S(1)} all-reduce(f32[4096]{0:T(1024)S(1)} %bitcast.32), channel_id=1, replica_groups=mesh['label'=64,'cent'=8] {'label'}, use_global_device_ids=true, to_apply=%region_10.0 | all-reduce | flops 4096 | bytes 32768 | tf_op jit(solution)/shard_map/psum | solution.py:26
  1142.9 0.6 fusion.10
  1143.5 451.7 %reduce-scatter.2.cloned.1.call-done = f32[64,256]{1,0:T(8,128)} async-done(((f32[4096,256]{1,0:T(8,128)}), f32[64,256]{1,0:T(8,128)}) %reduce-scatter.2.cloned.1.call-update) | async-done | bytes 65552 | tf_op jit(solution)/shard_map/reduce_scatter | solution.py:62
  1595.2 0.9 multiply_reduce_fusion
  1596.2 1.6 broadcast_multiply_fusion
  (15 shorter events, 0.1 us)
Async XLA Ops:
  7.2 1588.0 %reduce-scatter.2.cloned.1.call-start = ((), (), s32[]{:S(2)}) async-start(), calls=%async_computation.1 | async-start | bytes 4259840 | tf_op jit(solution)/shard_map/reduce_scatter | solution.py:62
  14.7 1.9 copy-start
  617.7 296.1 %copy-start.1 = (bf16[512,256]{1,0:T(8,128)(2,1)S(1)}, bf16[512,256]{1,0:T(8,128)(2,1)}, u32[]{:S(2)}) copy-start(bf16[512,256]{1,0:T(8,128)(2,1)} %param.3) | copy-start | bytes 786436
Sparse Core Ops, SparseCore 0:
  920.0 675.1 reduce-scatter.1
where the time goes:
time: 1620 us; the launch traced here: 1600 us
  blocking collectives  1090 us (67%)
  waiting for transfers between devices  452 us (28%)
  matrix products  38.5 us (2%)
    psum x4, blocking collectives, column_total(): summed = lax.psum(local_sum, 'label')  889 us
    reduce_scatter x1, waiting for transfers between devices, shards(): lax.psum_scatter(lax.dot_general(plan_weights, label_unit, (((0,), (0,)),...  452 us
    psum x3, blocking collectives, shards(): row_sum = lax.psum(row_local, 'cent')  202 us
  transfers between devices with their start and end apart: 1, of which 1 were waited for; matrix products, arithmetic and copies ran while one was open for 0% of the time, Pallas kernels for 0%

commit v1 on v0

v1 whole, which is shorter than its diff:
```python
import functools

import jax
import jax.numpy as jnp
from jax import lax
from jax.experimental import pallas as pl
from jax.experimental.pallas import tpu as pltpu
from jax.sharding import PartitionSpec as P

ITERS = 3
SOFTMAX_HEAT = 0.02
EPSILON = 1e-06

F32, BF16 = jnp.float32, jnp.bfloat16
MESH = pl.DeviceIdType.MESH
NT = (((1,), (1,)), ((), ()))

NY, NZ, NX, NK = 4, 16, 4, 2
LAB = 512
HALF = LAB // 2
WIDE = NY * LAB
KC = 4096
QUARTER = KC // NY
SIDE = WIDE // 2
FEAT = 256
BLOCK = QUARTER // NZ
TILE = 256
EXTRA = 8
CHUNKS = 2
PIECE = BLOCK // CHUNKS


def distance(offset, size):
    return min(offset, size - offset)


Y_OFFSETS = (2, 1, 3)
Z_OFFSETS = sorted(range(1, NZ), key=lambda d: -distance(d, NZ))
XY_OFFSETS = sorted(
    [(dy, dx) for dy in range(NY) for dx in range(NX) if dy or dx],
    key=lambda o: -(distance(o[0], NY) + distance(o[1], NX)),
)


def unit(values):
    wide = values.astype(F32)
    scale = lax.rsqrt(jnp.mean(wide * wide, axis=1, keepdims=True) + EPSILON)
    return (wide * scale).astype(BF16)


def gibbs(centroid_unit, label_unit):
    scores = lax.dot_general(centroid_unit, label_unit, NT, preferred_element_type=F32)
    return jnp.exp(scores * (1.0 / (SOFTMAX_HEAT * FEAT))).astype(BF16)


def split_rows(vector):
    high = vector.astype(BF16).astype(F32)
    rest = vector - high
    row = lax.broadcasted_iota(jnp.int32, (16, vector.shape[1]), 0)
    return jnp.where(row == 0, high, jnp.where(row == 1, rest, 0.0)).astype(BF16)


def joined(rows):
    return rows[0:1, :] + rows[1:2, :]


def kernel(
    counts_ref,
    lab_ref,
    cen_ref,
    new_ref,
    mass_ref,
    cen_unit,
    wide_gibbs,
    gibbs_t,
    lab_all,
    lab_send,
    lab_land,
    mask_all,
    row_scale,
    first_src,
    first_land,
    z_src,
    z_land,
    core_src,
    core_land,
    xy_src,
    xy_land,
    half_src,
    half_land,
    mass_src,
    mass_land,
    right_src,
    right_land,
    left_src,
    left_land,
    s_first, r_first,
    s_lab, r_lab,
    s_fwd, r_fwd,
    s_z, r_z,
    s_core, r_core,
    s_xy, r_xy,
    s_half, r_half,
    s_mass, r_mass,
    s_right, r_right,
    s_left, r_left,
):
    label, cent = lax.axis_index("label"), lax.axis_index("cent")
    y, z = label // NZ, lax.rem(label, NZ)
    x, k = cent // NK, lax.rem(cent, NK)
    other = 1 - k

    def at(dy=0, dz=0, dx=0):
        return (
            lax.rem(y + dy, NY) * NZ + lax.rem(z + dz, NZ),
            lax.rem(x + dx, NX) * NK + k,
        )

    partner = (label, x * NK + other)

    def send(src, dst, send_sem, recv_sem, device):
        pltpu.make_async_remote_copy(
            src_ref=src,
            dst_ref=dst,
            send_sem=send_sem,
            recv_sem=recv_sem,
            device_id=device,
            device_id_type=MESH,
        ).start()

    def arrived(dst, send_sem, recv_sem):
        pltpu.make_async_remote_copy(
            src_ref=dst,
            dst_ref=dst,
            send_sem=send_sem,
            recv_sem=recv_sem,
            device_id=partner,
            device_id_type=MESH,
        ).wait_recv()

    def sent(src, send_sem, recv_sem):
        pltpu.make_async_remote_copy(
            src_ref=src,
            dst_ref=src,
            send_sem=send_sem,
            recv_sem=recv_sem,
            device_id=partner,
            device_id_type=MESH,
        ).wait_send()

    barrier = pltpu.get_barrier_semaphore()
    for dz in Z_OFFSETS:
        pl.semaphore_signal(barrier, inc=1, device_id=at(dz=dz), device_id_type=MESH)
    for dy, dx in XY_OFFSETS:
        pl.semaphore_signal(
            barrier, inc=1, device_id=at(dy=dy, dx=dx), device_id_type=MESH
        )
    pl.semaphore_signal(barrier, inc=1, device_id=partner, device_id_type=MESH)

    count = counts_ref[0]
    own_rows = pl.multiple_of(y * LAB, LAB)
    for half in range(2):
        rows = slice(half * HALF, (half + 1) * HALF)
        unit_half = unit(lab_ref[rows, :])
        lab_all[pl.ds(own_rows + half * HALF, HALF), :] = unit_half
        lab_send[half, 0:HALF, :] = unit_half.astype(F32)
        slot = lax.broadcasted_iota(jnp.int32, (EXTRA, HALF), 1) + half * HALF
        lab_send[half, HALF : HALF + EXTRA, :] = jnp.where(slot < count, 1.0, 0.0)
    slot = lax.broadcasted_iota(jnp.int32, (16, LAB), 1)
    own_mask = jnp.where(slot < count, 1.0, 0.0)
    mask_all[:, pl.ds(own_rows, LAB)] = own_mask[0:1, :]
    own_mask = own_mask.astype(BF16)
    own_unit = lab_all[pl.ds(own_rows, LAB), :]

    for part in range(NY):
        def first_tile(j, _, part=part):
            rows = pl.ds(pl.multiple_of(part * QUARTER + j * TILE, TILE), TILE)
            tile_unit = unit(cen_ref[rows, :])
            cen_unit[rows, :] = tile_unit
            tile = gibbs(tile_unit, own_unit)
            wide_gibbs[rows, :] = tile
            sums = lax.dot_general(own_mask, tile, NT, preferred_element_type=F32)
            first_src[part, :, pl.ds(pl.multiple_of(j * TILE, TILE), TILE)] = sums[0:1, :]
            return 0

        lax.fori_loop(0, QUARTER // TILE, first_tile, 0)

    pl.semaphore_wait(barrier, NZ - 1 + NY * NX - 1 + 1)

    for dy in Y_OFFSETS:
        send(
            first_src.at[lax.rem(y + dy, NY)], first_land.at[dy - 1],
            s_first, r_first, at(dy=dy),
        )
    for dy in Y_OFFSETS:
        send(
            lab_send.at[k], lab_land.at[dy - 1, k],
            s_lab, r_lab.at[dy - 1], at(dy=dy),
        )

    def own_quarter(j, _):
        rows = pl.ds(pl.multiple_of(j * TILE, TILE), TILE)
        mine = pl.ds(pl.multiple_of(y * QUARTER + j * TILE, TILE), TILE)
        gibbs_t[rows, pl.ds(own_rows, LAB)] = wide_gibbs[mine, :]
        return 0

    lax.fori_loop(0, QUARTER // TILE, own_quarter, 0)

    def z_send(turn):
        for dz in Z_OFFSETS:
            send(z_src.at[turn], z_land.at[turn, dz - 1], s_z.at[turn], r_z.at[turn], at(dz=dz))

    def z_total(turn):
        arrived(z_land.at[turn], s_z.at[turn], r_z.at[turn])
        total = z_src[turn]
        for slot in range(NZ - 1):
            total = total + z_land[turn, slot]
        return total

    arrived(first_land, s_first, r_first)
    z_src[0] = first_src[y] + first_land[0] + first_land[1] + first_land[2]
    z_send(0)

    def take(dy, half):
        owner = lax.rem(y + (NY - dy), NY)
        rows = pl.ds(pl.multiple_of(owner * LAB + half * HALF, HALF), HALF)
        landed = lab_land[dy - 1, half, 0:HALF, :].astype(BF16)
        lab_all[rows, :] = landed
        mask_all[:, rows] = lab_land[dy - 1, half, HALF : HALF + 1, :]

        def tile(j, _):
            out = pl.ds(pl.multiple_of(j * TILE, TILE), TILE)
            mine = pl.ds(pl.multiple_of(y * QUARTER + j * TILE, TILE), TILE)
            gibbs_t[out, rows] = gibbs(cen_unit[mine, :], landed)
            return 0

        lax.fori_loop(0, QUARTER // TILE, tile, 0)

    for dy in (1, 3, 2):
        arrived(lab_land.at[dy - 1, k], s_lab, r_lab.at[dy - 1])
        send(
            lab_land.at[dy - 1, k], lab_land.at[dy - 1, k],
            s_fwd, r_fwd.at[dy - 1], partner,
        )
        take(dy, k)
    for dy in (1, 3, 2):
        arrived(lab_land.at[dy - 1, other], s_fwd, r_fwd.at[dy - 1])
        take(dy, other)

    def row_stage(turn, col_scale):
        scale_rows = split_rows(col_scale)
        for half in range(2):
            columns = slice(half * SIDE, (half + 1) * SIDE)
            core_src[turn, half] = joined(
                jnp.dot(scale_rows, gibbs_t[:, columns], preferred_element_type=F32)
            )
        send(core_src.at[turn, other], core_land.at[turn], s_core.at[turn], r_core.at[turn], partner)
        arrived(core_land.at[turn], s_core.at[turn], r_core.at[turn])
        xy_src[turn] = core_src[turn, k] + core_land[turn]
        for dy, dx in XY_OFFSETS:
            send(
                xy_src.at[turn], xy_land.at[turn, dy * NX + dx - 1],
                s_xy.at[turn], r_xy.at[turn], at(dy=dy, dx=dx),
            )
        arrived(xy_land.at[turn], s_xy.at[turn], r_xy.at[turn])
        total = xy_src[turn]
        for slot in range(NY * NX - 1):
            total = total + xy_land[turn, slot]
        mine = pl.ds(pl.multiple_of(k * SIDE, SIDE), SIDE)
        scale = mask_all[:, mine] / total
        half_src[turn] = scale
        send(half_src.at[turn], half_land.at[turn], s_half.at[turn], r_half.at[turn], partner)
        row_scale[:, mine] = scale
        arrived(half_land.at[turn], s_half.at[turn], r_half.at[turn])
        row_scale[:, pl.ds(pl.multiple_of(other * SIDE, SIDE), SIDE)] = half_land[turn]

    def col_stage(turn):
        scale_rows = split_rows(row_scale[...])
        for j in range(QUARTER // TILE):
            rows = slice(j * TILE, (j + 1) * TILE)
            z_src[turn, :, rows] = joined(
                lax.dot_general(scale_rows, gibbs_t[rows, :], NT, preferred_element_type=F32)
            )
        z_send(turn)

    col_scale = 1.0 / z_total(0)
    for turn in range(ITERS):
        if turn:
            col_stage(turn)
            col_scale = 1.0 / z_total(turn)
        row_stage(turn, col_scale)

    def block_stats(owner):
        rows = pl.ds(pl.multiple_of(owner * BLOCK, BLOCK), BLOCK)
        weights = (gibbs_t[rows, :].astype(F32) * row_scale[...]).astype(BF16)
        return jnp.dot(weights, lab_all[...], preferred_element_type=F32)

    to_right, to_left = at(dz=1), at(dz=NZ - 1)

    def pass_on(step, piece, src, land, s_sem, r_sem, device):
        send(src.at[step, piece], land.at[step, piece], s_sem, r_sem.at[step, piece], device)

    right = block_stats(lax.rem(z + 8, NZ))
    for piece in range(CHUNKS):
        right_src[0, piece] = right[piece * PIECE : (piece + 1) * PIECE, :]
        pass_on(0, piece, right_src, right_land, s_right, r_right, to_right)
    left = block_stats(lax.rem(z + NZ - 7, NZ))
    for piece in range(CHUNKS):
        left_src[0, piece] = left[piece * PIECE : (piece + 1) * PIECE, :]
        pass_on(0, piece, left_src, left_land, s_left, r_left, to_left)

    col_stage(ITERS)

    def ring_step(step, _):
        right = block_stats(lax.rem(z + 8 - step, NZ))
        left = block_stats(lax.rem(z + NZ - 7 + step, NZ))
        for piece in range(CHUNKS):
            part = slice(piece * PIECE, (piece + 1) * PIECE)
            arrived(right_land.at[step - 1, piece], s_right, r_right.at[step - 1, piece])
            right_src[step, piece] = right[part, :] + right_land[step - 1, piece]
            pass_on(step, piece, right_src, right_land, s_right, r_right, to_right)
            arrived(left_land.at[step - 1, piece], s_left, r_left.at[step - 1, piece])
            left_src[step, piece] = left[part, :] + left_land[step - 1, piece]
            pass_on(step, piece, left_src, left_land, s_left, r_left, to_left)
        return 0

    lax.fori_loop(1, 7, ring_step, 0)

    right = block_stats(lax.rem(z + 1, NZ))
    for piece in range(CHUNKS):
        part = slice(piece * PIECE, (piece + 1) * PIECE)
        arrived(right_land.at[6, piece], s_right, r_right.at[6, piece])
        right_src[7, piece] = right[part, :] + right_land[6, piece]
        pass_on(7, piece, right_src, right_land, s_right, r_right, to_right)

    mass = col_scale * z_total(ITERS)
    mass_src[...] = mass
    for dy in Y_OFFSETS:
        send(mass_src, mass_land.at[dy - 1], s_mass, r_mass, at(dy=dy))
    mass_ref[y] = mass

    own = block_stats(z)
    for piece in range(CHUNKS):
        part = slice(piece * PIECE, (piece + 1) * PIECE)
        arrived(left_land.at[6, piece], s_left, r_left.at[6, piece])
        arrived(right_land.at[7, piece], s_right, r_right.at[7, piece])
        stats = own[part, :] + left_land[6, piece] + right_land[7, piece]
        scale = lax.rsqrt(jnp.mean(stats * stats, axis=1, keepdims=True) + EPSILON)
        new_ref[part, :] = stats * scale

    arrived(mass_land, s_mass, r_mass)
    for dy in Y_OFFSETS:
        mass_ref[lax.rem(y + (NY - dy), NY)] = mass_land[dy - 1]

    sent(first_land, s_first, r_first)
    sent(lab_land.at[:, k], s_lab, r_lab.at[0])
    sent(lab_land.at[:, k], s_fwd, r_fwd.at[0])
    for turn in range(ITERS + 1):
        sent(z_land.at[turn], s_z.at[turn], r_z.at[turn])
    for turn in range(ITERS):
        sent(core_land.at[turn], s_core.at[turn], r_core.at[turn])
        sent(xy_land.at[turn], s_xy.at[turn], r_xy.at[turn])
        sent(half_land.at[turn], s_half.at[turn], r_half.at[turn])
    sent(mass_land, s_mass, r_mass)
    sent(right_src, s_right, r_right.at[0, 0])
    sent(left_src, s_left, r_left.at[0, 0])


def shards(labels, counts, centroids):
    vmem = pl.BlockSpec(memory_space=pltpu.VMEM)
    dma = pltpu.SemaphoreType.DMA
    new, mass = pl.pallas_call(
        kernel,
        out_shape=(
            jax.ShapeDtypeStruct((BLOCK, FEAT), F32),
            jax.ShapeDtypeStruct((NY, 1, QUARTER), F32),
        ),
        in_specs=[pl.BlockSpec(memory_space=pltpu.SMEM), vmem, vmem],
        out_specs=(vmem, vmem),
        scratch_shapes=[
            pltpu.VMEM((KC, FEAT), BF16),
            pltpu.VMEM((KC, LAB), BF16),
            pltpu.VMEM((QUARTER, WIDE), BF16),
            pltpu.VMEM((WIDE, FEAT), BF16),
            pltpu.VMEM((2, HALF + EXTRA, FEAT), F32),
            pltpu.VMEM((NY - 1, 2, HALF + EXTRA, FEAT), F32),
            pltpu.VMEM((1, WIDE), F32),
            pltpu.VMEM((1, WIDE), F32),
            pltpu.VMEM((NY, 1, QUARTER), F32),
            pltpu.VMEM((NY - 1, 1, QUARTER), F32),
            pltpu.VMEM((ITERS + 1, 1, QUARTER), F32),
            pltpu.VMEM((ITERS + 1, NZ - 1, 1, QUARTER), F32),
            pltpu.VMEM((ITERS, 2, 1, SIDE), F32),
            pltpu.VMEM((ITERS, 1, SIDE), F32),
            pltpu.VMEM((ITERS, 1, SIDE), F32),
            pltpu.VMEM((ITERS, NY * NX - 1, 1, SIDE), F32),
            pltpu.VMEM((ITERS, 1, SIDE), F32),
            pltpu.VMEM((ITERS, 1, SIDE), F32),
            pltpu.VMEM((1, QUARTER), F32),
            pltpu.VMEM((NY - 1, 1, QUARTER), F32),
            pltpu.VMEM((8, CHUNKS, PIECE, FEAT), F32),
            pltpu.VMEM((8, CHUNKS, PIECE, FEAT), F32),
            pltpu.VMEM((7, CHUNKS, PIECE, FEAT), F32),
            pltpu.VMEM((7, CHUNKS, PIECE, FEAT), F32),
            dma, dma,
            dma, dma((NY - 1,)),
            dma, dma((NY - 1,)),
            dma((ITERS + 1,)), dma((ITERS + 1,)),
            dma((ITERS,)), dma((ITERS,)),
            dma((ITERS,)), dma((ITERS,)),
            dma((ITERS,)), dma((ITERS,)),
            dma, dma,
            dma, dma((8, CHUNKS)),
            dma, dma((7, CHUNKS)),
        ],
        compiler_params=pltpu.CompilerParams(
            collective_id=0, has_side_effects=True, vmem_limit_bytes=48 << 20
        ),
        name="sinkhorn_assign",
    )(counts, labels, centroids)
    return new, mass.reshape(KC)


def solution(mesh):
    return jax.shard_map(
        shards,
        mesh=mesh,
        in_specs=(P("label", None), P("label"), P("cent", None)),
        out_specs=(P(("cent", "label"), None), P("cent")),
        check_vma=False,
    )
```

time: 1620 us -> 109 us (0.07)
  the two profiles are of different devices: /device:TPU:1 before, /device:TPU:2 now
where the time goes in v1:
time: 109 us; the launch traced here: 108 us
  Pallas kernels  103 us (94%)
  local copies, waits for them, and re-layouts  3.77 us (3%)
  between operations  1.29 us (1%)
    pallas_call x1, Pallas kernels, shards(): pl.pallas_call(kernel, out_shape=(jax.ShapeDtypeStruct((BLOCK, FEAT), F32...  103 us
    unnamed x6, local copies, waits for them, and re-layouts  3.77 us

profile of v1, /device:TPU:2, one launch (start us, length us, event | category | flops | bytes accessed | tf_op | source)
XLA Modules:
  0.0 108.5 jit_solution(18150958619528456929)
XLA Ops:
  1.3 0.0 copy-start
  1.3 1.6 %copy-done = bf16[4096,256]{1,0:T(8,128)(2,1)S(1)} copy-done((bf16[4096,256]{1,0:T(8,128)(2,1)S(1)}, bf16[4096,256]{1,0:T(8,128)(2,1)}, u32[]{:S(2)}) %copy-start) | copy-done | bytes 2097176
  2.9 0.0 copy-start.1
  2.9 0.9 copy-done.1
  3.8 103.4 %sinkhorn_assign.1 = (f32[64,256]{1,0:T(8,128)S(1)}, f32[4,1,1024]{2,1,0:T(1,128)S(1)}) custom-call(s32[1]{0:T(128)S(6)} %copy.7.counts_ref, bf16[512,256]{1,0:T(8,128)(2,1)S(1)} %copy-done.1, bf16[4096,256]{1,0:T(8,128)(2,1)S(1)} %copy-done), custom_call_target="tpu_custom_call" | custom-call | tf_op jit(solution)/shard_map/sinkhorn_assign/pallas_call | solution.py:372
  107.3 0.6 copy.8
  107.9 0.6 copy.9
Async XLA Ops:
  1.3 1.6 %copy-start = (bf16[4096,256]{1,0:T(8,128)(2,1)S(1)}, bf16[4096,256]{1,0:T(8,128)(2,1)}, u32[]{:S(2)}) copy-start(bf16[4096,256]{1,0:T(8,128)(2,1)} %cen_ref.1) | copy-start | bytes 6291460
  2.9 0.9 copy-start.1

commit v2 on v1

v2 whole, which is shorter than its diff:
```python
import functools
import math

import jax
import jax.numpy as jnp
from jax import lax
from jax.experimental import pallas as pl
from jax.experimental.pallas import tpu as pltpu
from jax.sharding import PartitionSpec as P

ITERS = 3
SOFTMAX_HEAT = 0.02
EPSILON = 1e-06

F32, BF16 = jnp.float32, jnp.bfloat16
MESH = pl.DeviceIdType.MESH
NT = (((1,), (1,)), ((), ()))

NY, NZ, NX, NK = 4, 16, 4, 2
LAB = 512
HALF = LAB // 2
WIDE = NY * LAB
KC = 4096
QUARTER = KC // NY
SIDE = WIDE // 2
FEAT = 256
BLOCK = QUARTER // NZ
TILE = 256
EXTRA = 8
CHUNKS = 2
STEPS = 4
PIECE = BLOCK // CHUNKS


def distance(offset, size):
    return min(offset, size - offset)


Y_OFFSETS = (2, 1, 3)
Z_OFFSETS = sorted(range(1, NZ), key=lambda d: -distance(d, NZ))
XY_OFFSETS = sorted(
    [(dy, dx) for dy in range(NY) for dx in range(NX) if dy or dx],
    key=lambda o: -(distance(o[0], NY) + distance(o[1], NX)),
)


XC_OFFSETS = sorted(
    [(dx, dk) for dx in range(NX) for dk in range(NK) if dx or dk],
    key=lambda o: -distance(o[0], NX),
)


def unit(values):
    wide = values.astype(F32)
    scale = lax.rsqrt(jnp.mean(wide * wide, axis=1, keepdims=True) + EPSILON)
    return (wide * scale).astype(BF16)


def gibbs(centroid_unit, label_unit):
    scores = lax.dot_general(centroid_unit, label_unit, NT, preferred_element_type=F32)
    return jnp.exp2(scores * (math.log2(math.e) / (SOFTMAX_HEAT * FEAT))).astype(BF16)


def split_rows(vector):
    high = vector.astype(BF16).astype(F32)
    rest = vector - high
    row = lax.broadcasted_iota(jnp.int32, (16, vector.shape[1]), 0)
    return jnp.where(row == 0, high, jnp.where(row == 1, rest, 0.0)).astype(BF16)


def joined(rows):
    return rows[0:1, :] + rows[1:2, :]


def kernel(
    counts_ref,
    lab_hbm,
    cen_hbm,
    new_ref,
    mass_ref,
    lab_ref,
    cen_ref,
    cen_unit,
    wide_gibbs,
    gibbs_t,
    lab_all,
    lab_send,
    lab_land,
    mask_all,
    row_scale,
    first_src,
    first_land,
    scale_src,
    scale_land,
    col_full,
    own_src,
    own_land,
    z_src,
    z_land,
    core_src,
    core_land,
    xy_src,
    xy_land,
    half_src,
    half_land,
    mass_src,
    mass_land,
    stat_src,
    stat_land,
    in_sem,
    s_first, r_first,
    s_lab, r_lab,
    s_fwd, r_fwd,
    s_z, r_z,
    s_core, r_core,
    s_xy, r_xy,
    s_half, r_half,
    s_mass, r_mass,
    s_scale, r_scale,
    s_own, r_own,
    s_stat, r_stat,
):
    label, cent = lax.axis_index("label"), lax.axis_index("cent")
    y, z = label // NZ, lax.rem(label, NZ)
    x, k = cent // NK, lax.rem(cent, NK)
    other = 1 - k

    copies = [pltpu.make_async_copy(lab_hbm, lab_ref, in_sem.at[NY])]
    for part in range(NY):
        rows = pl.ds(part * QUARTER, QUARTER)
        copies.append(
            pltpu.make_async_copy(cen_hbm.at[rows, :], cen_ref.at[rows, :], in_sem.at[part])
        )
    for copy in copies:
        copy.start()

    def at(dy=0, dz=0, dx=0, dk=0):
        return (
            lax.rem(y + dy, NY) * NZ + lax.rem(z + dz, NZ),
            lax.rem(x + dx, NX) * NK + lax.rem(k + dk, NK),
        )

    partner = (label, x * NK + other)

    def send(src, dst, send_sem, recv_sem, device):
        pltpu.make_async_remote_copy(
            src_ref=src,
            dst_ref=dst,
            send_sem=send_sem,
            recv_sem=recv_sem,
            device_id=device,
            device_id_type=MESH,
        ).start()

    def arrived(dst, send_sem, recv_sem):
        pltpu.make_async_remote_copy(
            src_ref=dst,
            dst_ref=dst,
            send_sem=send_sem,
            recv_sem=recv_sem,
            device_id=partner,
            device_id_type=MESH,
        ).wait_recv()

    def sent(src, send_sem, recv_sem):
        pltpu.make_async_remote_copy(
            src_ref=src,
            dst_ref=src,
            send_sem=send_sem,
            recv_sem=recv_sem,
            device_id=partner,
            device_id_type=MESH,
        ).wait_send()

    pending = []

    def sent_later(src, send_sem, recv_sem):
        pending.append(functools.partial(sent, src, send_sem, recv_sem))

    barrier = pltpu.get_barrier_semaphore()
    for dz in Z_OFFSETS:
        pl.semaphore_signal(barrier, inc=1, device_id=at(dz=dz), device_id_type=MESH)
    for dy, dx in XY_OFFSETS:
        pl.semaphore_signal(
            barrier, inc=1, device_id=at(dy=dy, dx=dx), device_id_type=MESH
        )
    for dx, dk in XC_OFFSETS:
        if dk:
            pl.semaphore_signal(
                barrier, inc=1, device_id=at(dx=dx, dk=dk), device_id_type=MESH
            )

    count = counts_ref[0]
    copies[0].wait()
    own_rows = pl.multiple_of(y * LAB, LAB)
    for half in range(2):
        rows = slice(half * HALF, (half + 1) * HALF)
        unit_half = unit(lab_ref[rows, :])
        lab_all[pl.ds(own_rows + half * HALF, HALF), :] = unit_half
        lab_send[half, 0:HALF, :] = unit_half.astype(F32)
        slot = lax.broadcasted_iota(jnp.int32, (EXTRA, HALF), 1) + half * HALF
        lab_send[half, HALF : HALF + EXTRA, :] = jnp.where(slot < count, 1.0, 0.0)
    slot = lax.broadcasted_iota(jnp.int32, (16, LAB), 1)
    own_mask = jnp.where(slot < count, 1.0, 0.0)
    mask_all[:, pl.ds(own_rows, LAB)] = own_mask[0:1, :]
    own_unit = lab_all[pl.ds(own_rows, LAB), :]

    def own_sums(turn, rows_of_scale, part, j, tile):
        sums = lax.dot_general(rows_of_scale, tile, NT, preferred_element_type=F32)
        first_src[turn, part, :, j * TILE : (j + 1) * TILE] = joined(sums)

    scale_rows = split_rows(own_mask[0:1, :])
    for part in range(NY):
        copies[part + 1].wait()
        for j in range(QUARTER // TILE):
            rows = slice(part * QUARTER + j * TILE, part * QUARTER + (j + 1) * TILE)
            tile_unit = unit(cen_ref[rows, :])
            cen_unit[rows, :] = tile_unit
            tile = gibbs(tile_unit, own_unit)
            wide_gibbs[rows, :] = tile
            own_sums(0, scale_rows, part, j, tile)

    pl.semaphore_wait(barrier, NZ - 1 + NY * NX - 1 + NX)

    def first_send(turn):
        for dy in Y_OFFSETS:
            send(
                first_src.at[turn, lax.rem(y + dy, NY)], first_land.at[turn, dy - 1],
                s_first.at[turn], r_first.at[turn], at(dy=dy),
            )
        sent_later(first_land.at[turn], s_first.at[turn], r_first.at[turn])

    def first_total(turn):
        arrived(first_land.at[turn], s_first.at[turn], r_first.at[turn])
        z_src[turn] = (
            first_src[turn, y] + first_land[turn, 0] + first_land[turn, 1] + first_land[turn, 2]
        )

    first_send(0)
    for dy in Y_OFFSETS:
        send(
            lab_send.at[k], lab_land.at[dy - 1, k],
            s_lab, r_lab.at[dy - 1], at(dy=dy),
        )
    sent_later(lab_land.at[:, k], s_lab, r_lab.at[0])

    def own_quarter(j, _):
        rows = pl.ds(pl.multiple_of(j * TILE, TILE), TILE)
        mine = pl.ds(pl.multiple_of(y * QUARTER + j * TILE, TILE), TILE)
        gibbs_t[rows, pl.ds(own_rows, LAB)] = wide_gibbs[mine, :]
        return 0

    lax.fori_loop(0, QUARTER // TILE, own_quarter, 0)

    def z_send(turn):
        for dz in Z_OFFSETS:
            send(z_src.at[turn], z_land.at[turn, dz - 1], s_z.at[turn], r_z.at[turn], at(dz=dz))
        sent_later(z_land.at[turn], s_z.at[turn], r_z.at[turn])

    def z_total(turn):
        arrived(z_land.at[turn], s_z.at[turn], r_z.at[turn])
        total = z_src[turn]
        for slot in range(NZ - 1):
            total = total + z_land[turn, slot]
        return total

    first_total(0)
    z_send(0)

    def take(dy, half):
        owner = lax.rem(y + (NY - dy), NY)
        rows = pl.ds(pl.multiple_of(owner * LAB + half * HALF, HALF), HALF)
        landed = lab_land[dy - 1, half, 0:HALF, :].astype(BF16)
        lab_all[rows, :] = landed
        mask_all[:, rows] = lab_land[dy - 1, half, HALF : HALF + 1, :]

        def tile(j, _):
            out = pl.ds(pl.multiple_of(j * TILE, TILE), TILE)
            mine = pl.ds(pl.multiple_of(y * QUARTER + j * TILE, TILE), TILE)
            gibbs_t[out, rows] = gibbs(cen_unit[mine, :], landed)
            return 0

        lax.fori_loop(0, QUARTER // TILE, tile, 0)

    def hand_over():
        for dy in (1, 3, 2):
            arrived(lab_land.at[dy - 1, k], s_lab, r_lab.at[dy - 1])
            send(
                lab_land.at[dy - 1, k], lab_land.at[dy - 1, k],
                s_fwd, r_fwd.at[dy - 1], partner,
            )
        sent_later(lab_land.at[:, k], s_fwd, r_fwd.at[0])

    def own_row_stage(col_scale):
        scale_src[...] = col_scale
        for dy in Y_OFFSETS:
            send(scale_src, scale_land.at[dy - 1], s_scale, r_scale, at(dy=dy))
        sent_later(scale_land, s_scale, r_scale)
        col_full[y] = col_scale
        arrived(scale_land, s_scale, r_scale)
        for dy in Y_OFFSETS:
            col_full[lax.rem(y + (NY - dy), NY)] = scale_land[dy - 1]
        sums = jnp.zeros((16, LAB), F32)
        for part in range(NY):
            rows = slice(part * QUARTER, (part + 1) * QUARTER)
            sums = sums + jnp.dot(
                split_rows(col_full[part]), wide_gibbs[rows, :], preferred_element_type=F32
            )
        own_src[...] = joined(sums)
        for dx, dk in XC_OFFSETS:
            send(
                own_src, own_land.at[dx * NK + dk - 1], s_own, r_own, at(dx=dx, dk=dk)
            )
        sent_later(own_land, s_own, r_own)
        hand_over()
        arrived(own_land, s_own, r_own)
        total = own_src[...]
        for slot in range(NX * NK - 1):
            total = total + own_land[slot]
        return own_mask[0:1, :] / total

    def row_stage(turn, col_scale):
        scale_rows = split_rows(col_scale)
        for half in range(2):
            columns = slice(half * SIDE, (half + 1) * SIDE)
            core_src[turn, half] = joined(
                jnp.dot(scale_rows, gibbs_t[:, columns], preferred_element_type=F32)
            )
        send(core_src.at[turn, other], core_land.at[turn], s_core.at[turn], r_core.at[turn], partner)
        sent_later(core_land.at[turn], s_core.at[turn], r_core.at[turn])
        arrived(core_land.at[turn], s_core.at[turn], r_core.at[turn])
        xy_src[turn] = core_src[turn, k] + core_land[turn]
        for dy, dx in XY_OFFSETS:
            send(
                xy_src.at[turn], xy_land.at[turn, dy * NX + dx - 1],
                s_xy.at[turn], r_xy.at[turn], at(dy=dy, dx=dx),
            )
        sent_later(xy_land.at[turn], s_xy.at[turn], r_xy.at[turn])
        arrived(xy_land.at[turn], s_xy.at[turn], r_xy.at[turn])
        total = xy_src[turn]
        for slot in range(NY * NX - 1):
            total = total + xy_land[turn, slot]
        mine = pl.ds(pl.multiple_of(k * SIDE, SIDE), SIDE)
        scale = mask_all[:, mine] / total
        half_src[turn] = scale
        send(half_src.at[turn], half_land.at[turn], s_half.at[turn], r_half.at[turn], partner)
        sent_later(half_land.at[turn], s_half.at[turn], r_half.at[turn])
        row_scale[:, mine] = scale
        arrived(half_land.at[turn], s_half.at[turn], r_half.at[turn])
        row_scale[:, pl.ds(pl.multiple_of(other * SIDE, SIDE), SIDE)] = half_land[turn]

    def col_stage(turn):
        scale_rows = split_rows(row_scale[...])
        for j in range(QUARTER // TILE):
            rows = slice(j * TILE, (j + 1) * TILE)
            z_src[turn, :, rows] = joined(
                lax.dot_general(scale_rows, gibbs_t[rows, :], NT, preferred_element_type=F32)
            )
        z_send(turn)

    col_scale = 1.0 / z_total(0)
    scale_rows = split_rows(own_row_stage(col_scale))
    for part in range(NY):
        for j in range(QUARTER // TILE):
            rows = slice(part * QUARTER + j * TILE, part * QUARTER + (j + 1) * TILE)
            own_sums(1, scale_rows, part, j, wide_gibbs[rows, :])
    first_send(1)
    for dy in (1, 3):
        take(dy, k)
    first_total(1)
    z_send(1)
    take(2, k)
    for dy in (1, 3, 2):
        arrived(lab_land.at[dy - 1, other], s_fwd, r_fwd.at[dy - 1])
        take(dy, other)
    for turn in range(1, ITERS):
        if turn > 1:
            col_stage(turn)
        col_scale = 1.0 / z_total(turn)
        row_stage(turn, col_scale)

    def block_stats(owner):
        rows = pl.ds(pl.multiple_of(owner * BLOCK, BLOCK), BLOCK)
        weights = (gibbs_t[rows, :].astype(F32) * row_scale[...]).astype(BF16)
        return jnp.dot(weights, lab_all[...], preferred_element_type=F32)

    chains = ((8, 1, 4), (7, -1, 4), (4, 1, 4), (3, -1, 3))

    def stat_step(step):
        for chain, (far, way, messages) in enumerate(chains):
            if step >= messages:
                continue
            away = way * (far - step) % NZ
            partial = block_stats(lax.rem(z + away, NZ))
            last = step == messages - 1
            device = at(dz=away if last else way % NZ)
            for piece in range(CHUNKS):
                value = partial[piece * PIECE : (piece + 1) * PIECE, :]
                if step:
                    arrived(
                        stat_land.at[chain, step - 1, piece],
                        s_stat.at[chain], r_stat.at[chain, step - 1, piece],
                    )
                    value = value + stat_land[chain, step - 1, piece]
                stat_src[chain, step, piece] = value
                send(
                    stat_src.at[chain, step, piece], stat_land.at[chain, step, piece],
                    s_stat.at[chain], r_stat.at[chain, step, piece], device,
                )

    stat_step(0)
    col_stage(ITERS)
    for step in range(1, STEPS):
        stat_step(step)
    for chain, (_, _, messages) in enumerate(chains):
        sent_later(stat_src.at[chain, 0:messages], s_stat.at[chain], r_stat.at[chain, 0, 0])

    mass = col_scale * z_total(ITERS)
    mass_src[...] = mass
    for dy in Y_OFFSETS:
        send(mass_src, mass_land.at[dy - 1], s_mass, r_mass, at(dy=dy))
    sent_later(mass_land, s_mass, r_mass)
    mass_ref[y] = mass

    own = block_stats(z)
    for piece in range(CHUNKS):
        part = slice(piece * PIECE, (piece + 1) * PIECE)
        stats = own[part, :]
        for chain in (3, 2, 1, 0):
            last = chains[chain][2] - 1
            arrived(
                stat_land.at[chain, last, piece], s_stat.at[chain], r_stat.at[chain, last, piece]
            )
            stats = stats + stat_land[chain, last, piece]
        scale = lax.rsqrt(jnp.mean(stats * stats, axis=1, keepdims=True) + EPSILON)
        new_ref[part, :] = stats * scale

    arrived(mass_land, s_mass, r_mass)
    for dy in Y_OFFSETS:
        mass_ref[lax.rem(y + (NY - dy), NY)] = mass_land[dy - 1]

    for wait in pending:
        wait()


def shards(labels, counts, centroids):
    vmem = pl.BlockSpec(memory_space=pltpu.VMEM)
    dma = pltpu.SemaphoreType.DMA
    new, mass = pl.pallas_call(
        kernel,
        out_shape=(
            jax.ShapeDtypeStruct((BLOCK, FEAT), F32),
            jax.ShapeDtypeStruct((NY, 1, QUARTER), F32),
        ),
        in_specs=[
            pl.BlockSpec(memory_space=pltpu.SMEM),
            pl.BlockSpec(memory_space=pl.ANY),
            pl.BlockSpec(memory_space=pl.ANY),
        ],
        out_specs=(vmem, vmem),
        scratch_shapes=[
            pltpu.VMEM((LAB, FEAT), BF16),
            pltpu.VMEM((KC, FEAT), BF16),
            pltpu.VMEM((KC, FEAT), BF16),
            pltpu.VMEM((KC, LAB), BF16),
            pltpu.VMEM((QUARTER, WIDE), BF16),
            pltpu.VMEM((WIDE, FEAT), BF16),
            pltpu.VMEM((2, HALF + EXTRA, FEAT), F32),
            pltpu.VMEM((NY - 1, 2, HALF + EXTRA, FEAT), F32),
            pltpu.VMEM((1, WIDE), F32),
            pltpu.VMEM((1, WIDE), F32),
            pltpu.VMEM((2, NY, 1, QUARTER), F32),
            pltpu.VMEM((2, NY - 1, 1, QUARTER), F32),
            pltpu.VMEM((1, QUARTER), F32),
            pltpu.VMEM((NY - 1, 1, QUARTER), F32),
            pltpu.VMEM((NY, 1, QUARTER), F32),
            pltpu.VMEM((1, LAB), F32),
            pltpu.VMEM((NX * NK - 1, 1, LAB), F32),
            pltpu.VMEM((ITERS + 1, 1, QUARTER), F32),
            pltpu.VMEM((ITERS + 1, NZ - 1, 1, QUARTER), F32),
            pltpu.VMEM((ITERS, 2, 1, SIDE), F32),
            pltpu.VMEM((ITERS, 1, SIDE), F32),
            pltpu.VMEM((ITERS, 1, SIDE), F32),
            pltpu.VMEM((ITERS, NY * NX - 1, 1, SIDE), F32),
            pltpu.VMEM((ITERS, 1, SIDE), F32),
            pltpu.VMEM((ITERS, 1, SIDE), F32),
            pltpu.VMEM((1, QUARTER), F32),
            pltpu.VMEM((NY - 1, 1, QUARTER), F32),
            pltpu.VMEM((4, STEPS, CHUNKS, PIECE, FEAT), F32),
            pltpu.VMEM((4, STEPS, CHUNKS, PIECE, FEAT), F32),
            dma((NY + 1,)),
            dma((2,)), dma((2,)),
            dma, dma((NY - 1,)),
            dma, dma((NY - 1,)),
            dma((ITERS + 1,)), dma((ITERS + 1,)),
            dma((ITERS,)), dma((ITERS,)),
            dma((ITERS,)), dma((ITERS,)),
            dma((ITERS,)), dma((ITERS,)),
            dma, dma,
            dma, dma,
            dma, dma,
            dma((4,)), dma((4, STEPS, CHUNKS)),
        ],
        compiler_params=pltpu.CompilerParams(
            collective_id=0, has_side_effects=True, vmem_limit_bytes=60 << 20
        ),
        name="sinkhorn_assign",
    )(counts, labels, centroids)
    return new, mass.reshape(KC)


def solution(mesh):
    return jax.shard_map(
        shards,
        mesh=mesh,
        in_specs=(P("label", None), P("label"), P("cent", None)),
        out_specs=(P(("cent", "label"), None), P("cent")),
        check_vma=False,
    )
```

time: 109 us -> 100 us (0.917)
  the two profiles are of different devices: /device:TPU:2 before, /device:TPU:1 now
where the time goes in v2:
time: 100 us
  Pallas kernels  96.2 us (96%)
  local copies, waits for them, and re-layouts  2.8 us (3%)
  between operations  1.28 us (1%)
    pallas_call x1, Pallas kernels, shards(): pl.pallas_call(kernel, out_shape=(jax.ShapeDtypeStruct((BLOCK, FEAT), F32...  96.2 us
    unnamed x2, local copies, waits for them, and re-layouts  2.8 us

profile of v2, /device:TPU:1, one launch (start us, length us, event | category | flops | bytes accessed | tf_op | source)
XLA Modules:
  0.0 100.2 jit_solution(12504475486662554414)
XLA Ops:
  1.3 96.2 %sinkhorn_assign.1 = (f32[64,256]{1,0:T(8,128)}, f32[4,1,1024]{2,1,0:T(1,128)}) custom-call(s32[1]{0:T(128)S(6)} %copy.7.counts_ref, bf16[512,256]{1,0:T(8,128)(2,1)} %lab_hbm.1, bf16[4096,256]{1,0:T(8,128)(2,1)} %cen_hbm.1), custom_call_target="tpu_custom_call" | custom-call | tf_op jit(solution)/shard_map/sinkhorn_assign/pallas_call | solution.py:449
  97.4 1.5 %copy.8 = f32[64,256]{1,0:T(8,128)} copy(f32[64,256]{1,0:T(8,128)} %get-tuple-element.8) | data formatting | bytes 131072
  98.9 1.3 %copy.9 = f32[4096]{0:T(1024)} copy(f32[4096]{0:T(1024)} %bitcast.1) | data formatting | bytes 32768

commit v3 on v2

--- a/solution.py
+++ b/solution.py
@@ -28,7 +28,8 @@
 TILE = 256
 EXTRA = 8
 CHUNKS = 2
-STEPS = 4
+CHAINS = ((8, 1, 4), (7, -1, 4), (4, 1, 4), (3, -1, 3))
+STEPS = max(messages for _, _, messages in CHAINS)
 PIECE = BLOCK // CHUNKS
 
 
@@ -37,6 +38,7 @@
 
 
 Y_OFFSETS = (2, 1, 3)
+PART_ORDER = (2, 1, 3, 0)
 Z_OFFSETS = sorted(range(1, NZ), key=lambda d: -distance(d, NZ))
 XY_OFFSETS = sorted(
     [(dy, dx) for dy in range(NY) for dx in range(NX) if dy or dx],
@@ -88,6 +90,7 @@
     lab_land,
     mask_all,
     row_scale,
+    weights,
     first_src,
     first_land,
     scale_src,
@@ -126,10 +129,10 @@
     other = 1 - k
 
     copies = [pltpu.make_async_copy(lab_hbm, lab_ref, in_sem.at[NY])]
-    for part in range(NY):
-        rows = pl.ds(part * QUARTER, QUARTER)
+    for dy in PART_ORDER:
+        rows = pl.ds(pl.multiple_of(lax.rem(y + dy, NY) * QUARTER, QUARTER), QUARTER)
         copies.append(
-            pltpu.make_async_copy(cen_hbm.at[rows, :], cen_ref.at[rows, :], in_sem.at[part])
+            pltpu.make_async_copy(cen_hbm.at[rows, :], cen_ref.at[rows, :], in_sem.at[dy])
         )
     for copy in copies:
         copy.start()
@@ -205,30 +208,31 @@
     mask_all[:, pl.ds(own_rows, LAB)] = own_mask[0:1, :]
     own_unit = lab_all[pl.ds(own_rows, LAB), :]
 
-    def own_sums(turn, rows_of_scale, part, j, tile):
-        sums = lax.dot_general(rows_of_scale, tile, NT, preferred_element_type=F32)
-        first_src[turn, part, :, j * TILE : (j + 1) * TILE] = joined(sums)
-
     scale_rows = split_rows(own_mask[0:1, :])
-    for part in range(NY):
-        copies[part + 1].wait()
+
+    def first_part(dy):
+        part = lax.rem(y + dy, NY)
+        copies[1 + PART_ORDER.index(dy)].wait()
         for j in range(QUARTER // TILE):
-            rows = slice(part * QUARTER + j * TILE, part * QUARTER + (j + 1) * TILE)
+            rows = pl.ds(pl.multiple_of(part * QUARTER + j * TILE, TILE), TILE)
             tile_unit = unit(cen_ref[rows, :])
             cen_unit[rows, :] = tile_unit
             tile = gibbs(tile_unit, own_unit)
             wide_gibbs[rows, :] = tile
-            own_sums(0, scale_rows, part, j, tile)
-
+            if dy == 0:
+                gibbs_t[j * TILE : (j + 1) * TILE, pl.ds(own_rows, LAB)] = tile
+            sums = lax.dot_general(scale_rows, tile, NT, preferred_element_type=F32)
+            first_src[0, part, :, j * TILE : (j + 1) * TILE] = joined(sums)
+
+    for dy in Y_OFFSETS:
+        first_part(dy)
     pl.semaphore_wait(barrier, NZ - 1 + NY * NX - 1 + NX)
 
-    def first_send(turn):
-        for dy in Y_OFFSETS:
-            send(
-                first_src.at[turn, lax.rem(y + dy, NY)], first_land.at[turn, dy - 1],
-                s_first.at[turn], r_first.at[turn], at(dy=dy),
-            )
-        sent_later(first_land.at[turn], s_first.at[turn], r_first.at[turn])
+    def first_send(turn, dy):
+        send(
+            first_src.at[turn, lax.rem(y + dy, NY)], first_land.at[turn, dy - 1],
+            s_first.at[turn], r_first.at[turn], at(dy=dy),
+        )
 
     def first_total(turn):
         arrived(first_land.at[turn], s_first.at[turn], r_first.at[turn])
@@ -236,21 +240,20 @@
             first_src[turn, y] + first_land[turn, 0] + first_land[turn, 1] + first_land[turn, 2]
         )
 
-    first_send(0)
-    for dy in Y_OFFSETS:
+    def lab_exchange(dy):
         send(
             lab_send.at[k], lab_land.at[dy - 1, k],
             s_lab, r_lab.at[dy - 1], at(dy=dy),
         )
+
+    for dy in Y_OFFSETS:
+        first_send(0, dy)
+    for dy in (1, 3):
+        lab_exchange(dy)
+    first_part(0)
+    for turn in range(2):
+        sent_later(first_land.at[turn], s_first.at[turn], r_first.at[turn])
     sent_later(lab_land.at[:, k], s_lab, r_lab.at[0])
-
-    def own_quarter(j, _):
-        rows = pl.ds(pl.multiple_of(j * TILE, TILE), TILE)
-        mine = pl.ds(pl.multiple_of(y * QUARTER + j * TILE, TILE), TILE)
-        gibbs_t[rows, pl.ds(own_rows, LAB)] = wide_gibbs[mine, :]
-        return 0
-
-    lax.fori_loop(0, QUARTER // TILE, own_quarter, 0)
 
     def z_send(turn):
         for dz in Z_OFFSETS:
@@ -282,14 +285,16 @@
 
         lax.fori_loop(0, QUARTER // TILE, tile, 0)
 
-    def hand_over():
-        for dy in (1, 3, 2):
-            arrived(lab_land.at[dy - 1, k], s_lab, r_lab.at[dy - 1])
-            send(
-                lab_land.at[dy - 1, k], lab_land.at[dy - 1, k],
-                s_fwd, r_fwd.at[dy - 1], partner,
-            )
-        sent_later(lab_land.at[:, k], s_fwd, r_fwd.at[0])
+    def hand_over(dy):
+        arrived(lab_land.at[dy - 1, k], s_lab, r_lab.at[dy - 1])
+        send(
+            lab_land.at[dy - 1, k], lab_land.at[dy - 1, k],
+            s_fwd, r_fwd.at[dy - 1], partner,
+        )
+
+    def other_after(dy):
+        arrived(lab_land.at[dy - 1, other], s_fwd, r_fwd.at[dy - 1])
+        return other
 
     def own_row_stage(col_scale):
         scale_src[...] = col_scale
@@ -297,7 +302,10 @@
             send(scale_src, scale_land.at[dy - 1], s_scale, r_scale, at(dy=dy))
         sent_later(scale_land, s_scale, r_scale)
         col_full[y] = col_scale
+        for dy in (1, 3):
+            hand_over(dy)
         arrived(scale_land, s_scale, r_scale)
+        lab_exchange(2)
         for dy in Y_OFFSETS:
             col_full[lax.rem(y + (NY - dy), NY)] = scale_land[dy - 1]
         sums = jnp.zeros((16, LAB), F32)
@@ -312,7 +320,8 @@
                 own_src, own_land.at[dx * NK + dk - 1], s_own, r_own, at(dx=dx, dk=dk)
             )
         sent_later(own_land, s_own, r_own)
-        hand_over()
+        take(1, k)
+        take(3, k)
         arrived(own_land, s_own, r_own)
         total = own_src[...]
         for slot in range(NX * NK - 1):
@@ -321,12 +330,15 @@
 
     def row_stage(turn, col_scale):
         scale_rows = split_rows(col_scale)
-        for half in range(2):
-            columns = slice(half * SIDE, (half + 1) * SIDE)
+        def half_sums(half):
+            columns = pl.ds(pl.multiple_of(half * SIDE, SIDE), SIDE)
             core_src[turn, half] = joined(
                 jnp.dot(scale_rows, gibbs_t[:, columns], preferred_element_type=F32)
             )
+
+        half_sums(other)
         send(core_src.at[turn, other], core_land.at[turn], s_core.at[turn], r_core.at[turn], partner)
+        half_sums(k)
         sent_later(core_land.at[turn], s_core.at[turn], r_core.at[turn])
         arrived(core_land.at[turn], s_core.at[turn], r_core.at[turn])
         xy_src[turn] = core_src[turn, k] + core_land[turn]
@@ -351,51 +363,56 @@
 
     def col_stage(turn):
         scale_rows = split_rows(row_scale[...])
-        for j in range(QUARTER // TILE):
-            rows = slice(j * TILE, (j + 1) * TILE)
-            z_src[turn, :, rows] = joined(
-                lax.dot_general(scale_rows, gibbs_t[rows, :], NT, preferred_element_type=F32)
-            )
+        z_src[turn] = joined(
+            lax.dot_general(scale_rows, gibbs_t[...], NT, preferred_element_type=F32)
+        )
         z_send(turn)
 
     col_scale = 1.0 / z_total(0)
     scale_rows = split_rows(own_row_stage(col_scale))
-    for part in range(NY):
-        for j in range(QUARTER // TILE):
-            rows = slice(part * QUARTER + j * TILE, part * QUARTER + (j + 1) * TILE)
-            own_sums(1, scale_rows, part, j, wide_gibbs[rows, :])
-    first_send(1)
-    for dy in (1, 3):
-        take(dy, k)
+    for dy in PART_ORDER:
+        part = lax.rem(y + dy, NY)
+        rows = pl.ds(pl.multiple_of(part * QUARTER, QUARTER), QUARTER)
+        first_src[1, part] = joined(
+            lax.dot_general(scale_rows, wide_gibbs[rows, :], NT, preferred_element_type=F32)
+        )
+        if dy:
+            first_send(1, dy)
+    take(1, other_after(1))
     first_total(1)
     z_send(1)
+    take(3, other_after(3))
+    hand_over(2)
+    sent_later(lab_land.at[:, k], s_fwd, r_fwd.at[0])
     take(2, k)
-    for dy in (1, 3, 2):
-        arrived(lab_land.at[dy - 1, other], s_fwd, r_fwd.at[dy - 1])
-        take(dy, other)
+    take(2, other_after(2))
     for turn in range(1, ITERS):
         if turn > 1:
             col_stage(turn)
         col_scale = 1.0 / z_total(turn)
         row_stage(turn, col_scale)
 
-    def block_stats(owner):
-        rows = pl.ds(pl.multiple_of(owner * BLOCK, BLOCK), BLOCK)
-        weights = (gibbs_t[rows, :].astype(F32) * row_scale[...]).astype(BF16)
-        return jnp.dot(weights, lab_all[...], preferred_element_type=F32)
-
-    chains = ((8, 1, 4), (7, -1, 4), (4, 1, 4), (3, -1, 3))
+    def block_stats(offsets):
+        for slot, offset in enumerate(offsets):
+            owner = lax.rem(z + offset, NZ)
+            rows = pl.ds(pl.multiple_of(owner * BLOCK, BLOCK), BLOCK)
+            weights[slot * BLOCK : (slot + 1) * BLOCK, :] = (
+                gibbs_t[rows, :].astype(F32) * row_scale[...]
+            ).astype(BF16)
+        return jnp.dot(
+            weights[0 : len(offsets) * BLOCK, :], lab_all[...], preferred_element_type=F32
+        )
 
     def stat_step(step):
-        for chain, (far, way, messages) in enumerate(chains):
-            if step >= messages:
-                continue
-            away = way * (far - step) % NZ
-            partial = block_stats(lax.rem(z + away, NZ))
-            last = step == messages - 1
-            device = at(dz=away if last else way % NZ)
+        active = [c for c, (_, _, messages) in enumerate(CHAINS) if step < messages]
+        away = [CHAINS[c][1] * (CHAINS[c][0] - step) % NZ for c in active]
+        partial = block_stats(away + [0] * (step == STEPS - 1))
+        for slot, chain in enumerate(active):
+            _, way, messages = CHAINS[chain]
+            device = at(dz=away[slot] if step == messages - 1 else way % NZ)
             for piece in range(CHUNKS):
-                value = partial[piece * PIECE : (piece + 1) * PIECE, :]
+                start = slot * BLOCK + piece * PIECE
+                value = partial[start : start + PIECE, :]
                 if step:
                     arrived(
                         stat_land.at[chain, step - 1, piece],
@@ -407,12 +424,13 @@
                     stat_src.at[chain, step, piece], stat_land.at[chain, step, piece],
                     s_stat.at[chain], r_stat.at[chain, step, piece], device,
                 )
+        return partial[len(active) * BLOCK :, :]
 
     stat_step(0)
     col_stage(ITERS)
     for step in range(1, STEPS):
-        stat_step(step)
-    for chain, (_, _, messages) in enumerate(chains):
+        own = stat_step(step)
+    for chain, (_, _, messages) in enumerate(CHAINS):
         sent_later(stat_src.at[chain, 0:messages], s_stat.at[chain], r_stat.at[chain, 0, 0])
 
     mass = col_scale * z_total(ITERS)
@@ -422,12 +440,11 @@
     sent_later(mass_land, s_mass, r_mass)
     mass_ref[y] = mass
 
-    own = block_stats(z)
     for piece in range(CHUNKS):
         part = slice(piece * PIECE, (piece + 1) * PIECE)
         stats = own[part, :]
-        for chain in (3, 2, 1, 0):
-            last = chains[chain][2] - 1
+        for chain in reversed(range(len(CHAINS))):
+            last = CHAINS[chain][2] - 1
             arrived(
                 stat_land.at[chain, last, piece], s_stat.at[chain], r_stat.at[chain, last, piece]
             )
@@ -469,6 +486,7 @@
             pltpu.VMEM((NY - 1, 2, HALF + EXTRA, FEAT), F32),
             pltpu.VMEM((1, WIDE), F32),
             pltpu.VMEM((1, WIDE), F32),
+            pltpu.VMEM(((len(CHAINS) + 1) * BLOCK, WIDE), BF16),
             pltpu.VMEM((2, NY, 1, QUARTER), F32),
             pltpu.VMEM((2, NY - 1, 1, QUARTER), F32),
             pltpu.VMEM((1, QUARTER), F32),
@@ -486,8 +504,8 @@
             pltpu.VMEM((ITERS, 1, SIDE), F32),
             pltpu.VMEM((1, QUARTER), F32),
             pltpu.VMEM((NY - 1, 1, QUARTER), F32),
-            pltpu.VMEM((4, STEPS, CHUNKS, PIECE, FEAT), F32),
-            pltpu.VMEM((4, STEPS, CHUNKS, PIECE, FEAT), F32),
+            pltpu.VMEM((len(CHAINS), STEPS, CHUNKS, PIECE, FEAT), F32),
+            pltpu.VMEM((len(CHAINS), STEPS, CHUNKS, PIECE, FEAT), F32),
             dma((NY + 1,)),
             dma((2,)), dma((2,)),
             dma, dma((NY - 1,)),
@@ -499,10 +517,10 @@
             dma, dma,
             dma, dma,
             dma, dma,
-            dma((4,)), dma((4, STEPS, CHUNKS)),
+            dma((len(CHAINS),)), dma((len(CHAINS), STEPS, CHUNKS)),
         ],
         compiler_params=pltpu.CompilerParams(
-            collective_id=0, has_side_effects=True, vmem_limit_bytes=60 << 20
+            collective_id=0, has_side_effects=True, vmem_limit_bytes=55040 << 10
         ),
         name="sinkhorn_assign",
     )(counts, labels, centroids)

time: 100 us -> 94.3 us (0.943)
  Pallas kernels: 96.2 us -> 91.4 us
  local copies, waits for them, and re-layouts: 2.8 us -> 1.24 us
    pallas_call x1, Pallas kernels: 96.2 us -> 91.4 us  [shards(): pl.pallas_call(kernel, out_shape=(jax.ShapeDtypeStruct((BLOCK, FEAT), F32...]
    unnamed x2, local copies, waits for them, and re-layouts: 2.8 us -> 1.24 us
where the time goes in v3:
time: 94.3 us; the launch traced here: 93.9 us
  Pallas kernels  91.4 us (97%)
  between operations  1.28 us (1%)
  local copies, waits for them, and re-layouts  1.24 us (1%)
    pallas_call x1, Pallas kernels, shards(): pl.pallas_call(kernel, out_shape=(jax.ShapeDtypeStruct((BLOCK, FEAT), F32...  91.4 us

profile of v3, /device:TPU:1, one launch (start us, length us, event | category | flops | bytes accessed | tf_op | source)
XLA Modules:
  0.0 93.9 jit_solution(5586854650688352158)
XLA Ops:
  1.3 91.4 %sinkhorn_assign.1 = (f32[64,256]{1,0:T(8,128)S(1)}, f32[4,1,1024]{2,1,0:T(1,128)S(1)}) custom-call(s32[1]{0:T(128)S(6)} %copy.7.counts_ref, bf16[512,256]{1,0:T(8,128)(2,1)} %lab_hbm.1, bf16[4096,256]{1,0:T(8,128)(2,1)} %cen_hbm.1), custom_call_target="tpu_custom_call" | custom-call | tf_op jit(solution)/shard_map/sinkhorn_assign/pallas_call | solution.py:466
  92.6 0.6 copy.8
  93.3 0.6 copy.9

commit v4 on v3

--- a/solution.py
+++ b/solution.py
@@ -392,27 +392,29 @@
         col_scale = 1.0 / z_total(turn)
         row_stage(turn, col_scale)
 
-    def block_stats(offsets):
+    def block_stats(offsets, piece):
         for slot, offset in enumerate(offsets):
             owner = lax.rem(z + offset, NZ)
-            rows = pl.ds(pl.multiple_of(owner * BLOCK, BLOCK), BLOCK)
-            weights[slot * BLOCK : (slot + 1) * BLOCK, :] = (
+            rows = pl.ds(pl.multiple_of(owner * BLOCK + piece * PIECE, PIECE), PIECE)
+            weights[piece, slot * PIECE : (slot + 1) * PIECE, :] = (
                 gibbs_t[rows, :].astype(F32) * row_scale[...]
             ).astype(BF16)
         return jnp.dot(
-            weights[0 : len(offsets) * BLOCK, :], lab_all[...], preferred_element_type=F32
+            weights[piece, 0 : len(offsets) * PIECE, :],
+            lab_all[...],
+            preferred_element_type=F32,
         )
 
     def stat_step(step):
         active = [c for c, (_, _, messages) in enumerate(CHAINS) if step < messages]
         away = [CHAINS[c][1] * (CHAINS[c][0] - step) % NZ for c in active]
-        partial = block_stats(away + [0] * (step == STEPS - 1))
-        for slot, chain in enumerate(active):
-            _, way, messages = CHAINS[chain]
-            device = at(dz=away[slot] if step == messages - 1 else way % NZ)
-            for piece in range(CHUNKS):
-                start = slot * BLOCK + piece * PIECE
-                value = partial[start : start + PIECE, :]
+        rest = []
+        for piece in range(CHUNKS):
+            partial = block_stats(away + [0] * (step == STEPS - 1), piece)
+            for slot, chain in enumerate(active):
+                _, way, messages = CHAINS[chain]
+                device = at(dz=away[slot] if step == messages - 1 else way % NZ)
+                value = partial[slot * PIECE : (slot + 1) * PIECE, :]
                 if step:
                     arrived(
                         stat_land.at[chain, step - 1, piece],
@@ -424,10 +426,15 @@
                     stat_src.at[chain, step, piece], stat_land.at[chain, step, piece],
                     s_stat.at[chain], r_stat.at[chain, step, piece], device,
                 )
-        return partial[len(active) * BLOCK :, :]
+            rest.append(partial[len(active) * PIECE :, :])
+        return rest
 
     stat_step(0)
     col_stage(ITERS)
+    last_sends = pending.pop()
+    for wait in pending:
+        wait()
+    pending[:] = [last_sends]
     for step in range(1, STEPS):
         own = stat_step(step)
     for chain, (_, _, messages) in enumerate(CHAINS):
@@ -442,7 +449,7 @@
 
     for piece in range(CHUNKS):
         part = slice(piece * PIECE, (piece + 1) * PIECE)
-        stats = own[part, :]
+        stats = own[piece]
         for chain in reversed(range(len(CHAINS))):
             last = CHAINS[chain][2] - 1
             arrived(
@@ -486,7 +493,7 @@
             pltpu.VMEM((NY - 1, 2, HALF + EXTRA, FEAT), F32),
             pltpu.VMEM((1, WIDE), F32),
             pltpu.VMEM((1, WIDE), F32),
-            pltpu.VMEM(((len(CHAINS) + 1) * BLOCK, WIDE), BF16),
+            pltpu.VMEM((CHUNKS, (len(CHAINS) + 1) * PIECE, WIDE), BF16),
             pltpu.VMEM((2, NY, 1, QUARTER), F32),
             pltpu.VMEM((2, NY - 1, 1, QUARTER), F32),
             pltpu.VMEM((1, QUARTER), F32),

time: 94.3 us -> 94.4 us (level); the launches traced: 93.9 us -> 92.5 us
  Pallas kernels: 91.4 us -> 90 us
    pallas_call x1, Pallas kernels: 91.4 us -> 90 us  [shards(): pl.pallas_call(kernel, out_shape=(jax.ShapeDtypeStruct((BLOCK, FEAT), F32...]
where the time goes in v4:
time: 94.4 us; the launch traced here: 92.5 us
  Pallas kernels  90 us (95%)
  between operations  1.28 us (1%)
  local copies, waits for them, and re-layouts  1.24 us (1%)
    pallas_call x1, Pallas kernels, shards(): pl.pallas_call(kernel, out_shape=(jax.ShapeDtypeStruct((BLOCK, FEAT), F32...  90 us

profile of v4, /device:TPU:1, one launch (start us, length us, event | category | flops | bytes accessed | tf_op | source)
XLA Modules:
  0.0 92.5 jit_solution(2281732233656979926)
XLA Ops:
  1.3 90.0 %sinkhorn_assign.1 = (f32[64,256]{1,0:T(8,128)S(1)}, f32[4,1,1024]{2,1,0:T(1,128)S(1)}) custom-call(s32[1]{0:T(128)S(6)} %copy.7.counts_ref, bf16[512,256]{1,0:T(8,128)(2,1)} %lab_hbm.1, bf16[4096,256]{1,0:T(8,128)(2,1)} %cen_hbm.1), custom_call_target="tpu_custom_call" | custom-call | tf_op jit(solution)/shard_map/sinkhorn_assign/pallas_call | solution.py:473
  91.3 0.6 copy.8
  91.9 0.6 copy.9

commit v5 on v4

--- a/solution.py
+++ b/solution.py
@@ -31,6 +31,7 @@
 CHAINS = ((8, 1, 4), (7, -1, 4), (4, 1, 4), (3, -1, 3))
 STEPS = max(messages for _, _, messages in CHAINS)
 PIECE = BLOCK // CHUNKS
+SHARE = HALF // NX
 
 
 def distance(offset, size):
@@ -46,10 +47,7 @@
 )
 
 
-XC_OFFSETS = sorted(
-    [(dx, dk) for dx in range(NX) for dk in range(NK) if dx or dk],
-    key=lambda o: -distance(o[0], NX),
-)
+X_OFFSETS = (2, 1, 3)
 
 
 def unit(values):
@@ -93,11 +91,10 @@
     weights,
     first_src,
     first_land,
-    scale_src,
-    scale_land,
-    col_full,
-    own_src,
-    own_land,
+    far_land,
+    far_x,
+    far_core,
+    far_mask,
     z_src,
     z_land,
     core_src,
@@ -119,8 +116,11 @@
     s_xy, r_xy,
     s_half, r_half,
     s_mass, r_mass,
-    s_scale, r_scale,
-    s_own, r_own,
+    s_far, r_far,
+    s_far_x, r_far_x,
+    s_far_core, r_far_core,
+    s_far_rest, r_far_rest,
+    s_far_mask, r_far_mask,
     s_stat, r_stat,
 ):
     label, cent = lax.axis_index("label"), lax.axis_index("cent")
@@ -137,10 +137,10 @@
     for copy in copies:
         copy.start()
 
-    def at(dy=0, dz=0, dx=0, dk=0):
+    def at(dy=0, dz=0, dx=0):
         return (
             lax.rem(y + dy, NY) * NZ + lax.rem(z + dz, NZ),
-            lax.rem(x + dx, NX) * NK + lax.rem(k + dk, NK),
+            lax.rem(x + dx, NX) * NK + k,
         )
 
     partner = (label, x * NK + other)
@@ -187,11 +187,7 @@
         pl.semaphore_signal(
             barrier, inc=1, device_id=at(dy=dy, dx=dx), device_id_type=MESH
         )
-    for dx, dk in XC_OFFSETS:
-        if dk:
-            pl.semaphore_signal(
-                barrier, inc=1, device_id=at(dx=dx, dk=dk), device_id_type=MESH
-            )
+    pl.semaphore_signal(barrier, inc=1, device_id=partner, device_id_type=MESH)
 
     count = counts_ref[0]
     copies[0].wait()
@@ -222,37 +218,34 @@
             if dy == 0:
                 gibbs_t[j * TILE : (j + 1) * TILE, pl.ds(own_rows, LAB)] = tile
             sums = lax.dot_general(scale_rows, tile, NT, preferred_element_type=F32)
-            first_src[0, part, :, j * TILE : (j + 1) * TILE] = joined(sums)
+            first_src[part, :, j * TILE : (j + 1) * TILE] = joined(sums)
 
     for dy in Y_OFFSETS:
         first_part(dy)
-    pl.semaphore_wait(barrier, NZ - 1 + NY * NX - 1 + NX)
-
-    def first_send(turn, dy):
-        send(
-            first_src.at[turn, lax.rem(y + dy, NY)], first_land.at[turn, dy - 1],
-            s_first.at[turn], r_first.at[turn], at(dy=dy),
-        )
-
-    def first_total(turn):
-        arrived(first_land.at[turn], s_first.at[turn], r_first.at[turn])
-        z_src[turn] = (
-            first_src[turn, y] + first_land[turn, 0] + first_land[turn, 1] + first_land[turn, 2]
-        )
+    pl.semaphore_wait(barrier, NZ - 1 + NY * NX - 1 + 1)
 
     def lab_exchange(dy):
         send(
-            lab_send.at[k], lab_land.at[dy - 1, k],
-            s_lab, r_lab.at[dy - 1], at(dy=dy),
+            lab_send.at[k], lab_land.at[dy // 2, k],
+            s_lab, r_lab.at[dy // 2], at(dy=dy),
         )
 
     for dy in Y_OFFSETS:
-        first_send(0, dy)
+        send(
+            first_src.at[lax.rem(y + dy, NY)], first_land.at[dy - 1],
+            s_first, r_first, at(dy=dy),
+        )
+    send(
+        lab_send.at[k, pl.ds(pl.multiple_of(x * SHARE, SHARE), SHARE), :], far_land,
+        s_far, r_far, at(dy=2),
+    )
+    send(lab_send.at[:, HALF : HALF + EXTRA, :], far_mask, s_far_mask, r_far_mask, at(dy=2))
     for dy in (1, 3):
         lab_exchange(dy)
     first_part(0)
-    for turn in range(2):
-        sent_later(first_land.at[turn], s_first.at[turn], r_first.at[turn])
+    sent_later(first_land, s_first, r_first)
+    sent_later(far_land, s_far, r_far)
+    sent_later(far_mask, s_far_mask, r_far_mask)
     sent_later(lab_land.at[:, k], s_lab, r_lab.at[0])
 
     def z_send(turn):
@@ -267,66 +260,65 @@
             total = total + z_land[turn, slot]
         return total
 
-    first_total(0)
+    arrived(first_land, s_first, r_first)
+    z_src[0] = first_src[y] + first_land[0] + first_land[1] + first_land[2]
     z_send(0)
+
+    arrived(far_land, s_far, r_far)
+    for dx in X_OFFSETS:
+        send(far_land, far_x.at[dx - 1], s_far_x, r_far_x, at(dx=dx))
+    send(far_land, far_core.at[0], s_far_core, r_far_core, partner)
+    sent_later(far_x, s_far_x, r_far_x)
+    sent_later(far_land, s_far_core, r_far_core)
+
+    def fill(owner, half):
+        rows = pl.ds(pl.multiple_of(owner * LAB + half * HALF, HALF), HALF)
+        for j in range(QUARTER // TILE):
+            mine = pl.ds(pl.multiple_of(y * QUARTER + j * TILE, TILE), TILE)
+            gibbs_t[j * TILE : (j + 1) * TILE, rows] = gibbs(cen_unit[mine, :], lab_all[rows, :])
 
     def take(dy, half):
         owner = lax.rem(y + (NY - dy), NY)
         rows = pl.ds(pl.multiple_of(owner * LAB + half * HALF, HALF), HALF)
-        landed = lab_land[dy - 1, half, 0:HALF, :].astype(BF16)
-        lab_all[rows, :] = landed
-        mask_all[:, rows] = lab_land[dy - 1, half, HALF : HALF + 1, :]
-
-        def tile(j, _):
-            out = pl.ds(pl.multiple_of(j * TILE, TILE), TILE)
-            mine = pl.ds(pl.multiple_of(y * QUARTER + j * TILE, TILE), TILE)
-            gibbs_t[out, rows] = gibbs(cen_unit[mine, :], landed)
-            return 0
-
-        lax.fori_loop(0, QUARTER // TILE, tile, 0)
+        lab_all[rows, :] = lab_land[dy // 2, half, 0:HALF, :].astype(BF16)
+        mask_all[:, rows] = lab_land[dy // 2, half, HALF : HALF + 1, :]
+        fill(owner, half)
+
+    def take_far(half, quarters):
+        owner = lax.rem(y + 2, NY)
+        start = owner * LAB + half * HALF
+        for dx, quarter in enumerate(quarters):
+            first = start + lax.rem(x + (NX - dx), NX) * SHARE
+            lab_all[pl.ds(pl.multiple_of(first, SHARE), SHARE), :] = quarter[...].astype(BF16)
+        mask_all[:, pl.ds(pl.multiple_of(start, HALF), HALF)] = far_mask[half, 0:1, :]
+        fill(owner, half)
 
     def hand_over(dy):
-        arrived(lab_land.at[dy - 1, k], s_lab, r_lab.at[dy - 1])
+        arrived(lab_land.at[dy // 2, k], s_lab, r_lab.at[dy // 2])
         send(
-            lab_land.at[dy - 1, k], lab_land.at[dy - 1, k],
-            s_fwd, r_fwd.at[dy - 1], partner,
+            lab_land.at[dy // 2, k], lab_land.at[dy // 2, k],
+            s_fwd, r_fwd.at[dy // 2], partner,
         )
 
     def other_after(dy):
-        arrived(lab_land.at[dy - 1, other], s_fwd, r_fwd.at[dy - 1])
+        arrived(lab_land.at[dy // 2, other], s_fwd, r_fwd.at[dy // 2])
         return other
 
-    def own_row_stage(col_scale):
-        scale_src[...] = col_scale
-        for dy in Y_OFFSETS:
-            send(scale_src, scale_land.at[dy - 1], s_scale, r_scale, at(dy=dy))
-        sent_later(scale_land, s_scale, r_scale)
-        col_full[y] = col_scale
-        for dy in (1, 3):
-            hand_over(dy)
-        arrived(scale_land, s_scale, r_scale)
-        lab_exchange(2)
-        for dy in Y_OFFSETS:
-            col_full[lax.rem(y + (NY - dy), NY)] = scale_land[dy - 1]
-        sums = jnp.zeros((16, LAB), F32)
-        for part in range(NY):
-            rows = slice(part * QUARTER, (part + 1) * QUARTER)
-            sums = sums + jnp.dot(
-                split_rows(col_full[part]), wide_gibbs[rows, :], preferred_element_type=F32
-            )
-        own_src[...] = joined(sums)
-        for dx, dk in XC_OFFSETS:
-            send(
-                own_src, own_land.at[dx * NK + dk - 1], s_own, r_own, at(dx=dx, dk=dk)
-            )
-        sent_later(own_land, s_own, r_own)
-        take(1, k)
-        take(3, k)
-        arrived(own_land, s_own, r_own)
-        total = own_src[...]
-        for slot in range(NX * NK - 1):
-            total = total + own_land[slot]
-        return own_mask[0:1, :] / total
+    for dy in (1, 3):
+        hand_over(dy)
+    arrived(far_x, s_far_x, r_far_x)
+    send(far_x, far_core.at[1:NX], s_far_rest, r_far_rest, partner)
+    sent_later(lab_land.at[:, k], s_fwd, r_fwd.at[0])
+    sent_later(far_x, s_far_rest, r_far_rest)
+    take(1, k)
+    take(3, k)
+    arrived(far_mask, s_far_mask, r_far_mask)
+    take_far(k, [far_land] + [far_x.at[dx - 1] for dx in range(1, NX)])
+    for dy in (1, 3):
+        take(dy, other_after(dy))
+    arrived(far_core.at[0], s_far_core, r_far_core)
+    arrived(far_core.at[1:NX], s_far_rest, r_far_rest)
+    take_far(other, [far_core.at[dx] for dx in range(NX)])
 
     def row_stage(turn, col_scale):
         scale_rows = split_rows(col_scale)
@@ -369,27 +361,10 @@
         z_send(turn)
 
     col_scale = 1.0 / z_total(0)
-    scale_rows = split_rows(own_row_stage(col_scale))
-    for dy in PART_ORDER:
-        part = lax.rem(y + dy, NY)
-        rows = pl.ds(pl.multiple_of(part * QUARTER, QUARTER), QUARTER)
-        first_src[1, part] = joined(
-            lax.dot_general(scale_rows, wide_gibbs[rows, :], NT, preferred_element_type=F32)
-        )
-        if dy:
-            first_send(1, dy)
-    take(1, other_after(1))
-    first_total(1)
-    z_send(1)
-    take(3, other_after(3))
-    hand_over(2)
-    sent_later(lab_land.at[:, k], s_fwd, r_fwd.at[0])
-    take(2, k)
-    take(2, other_after(2))
-    for turn in range(1, ITERS):
-        if turn > 1:
+    for turn in range(ITERS):
+        if turn:
             col_stage(turn)
-        col_scale = 1.0 / z_total(turn)
+            col_scale = 1.0 / z_total(turn)
         row_stage(turn, col_scale)
 
     def block_stats(offsets, piece):
@@ -490,17 +465,16 @@
             pltpu.VMEM((QUARTER, WIDE), BF16),
             pltpu.VMEM((WIDE, FEAT), BF16),
             pltpu.VMEM((2, HALF + EXTRA, FEAT), F32),
-            pltpu.VMEM((NY - 1, 2, HALF + EXTRA, FEAT), F32),
+            pltpu.VMEM((2, 2, HALF + EXTRA, FEAT), F32),
             pltpu.VMEM((1, WIDE), F32),
             pltpu.VMEM((1, WIDE), F32),
             pltpu.VMEM((CHUNKS, (len(CHAINS) + 1) * PIECE, WIDE), BF16),
-            pltpu.VMEM((2, NY, 1, QUARTER), F32),
-            pltpu.VMEM((2, NY - 1, 1, QUARTER), F32),
-            pltpu.VMEM((1, QUARTER), F32),
+            pltpu.VMEM((NY, 1, QUARTER), F32),
             pltpu.VMEM((NY - 1, 1, QUARTER), F32),
-            pltpu.VMEM((NY, 1, QUARTER), F32),
-            pltpu.VMEM((1, LAB), F32),
-            pltpu.VMEM((NX * NK - 1, 1, LAB), F32),
+            pltpu.VMEM((SHARE, FEAT), F32),
+            pltpu.VMEM((NX - 1, SHARE, FEAT), F32),
+            pltpu.VMEM((NX, SHARE, FEAT), F32),
+            pltpu.VMEM((2, EXTRA, FEAT), F32),
             pltpu.VMEM((ITERS + 1, 1, QUARTER), F32),
             pltpu.VMEM((ITERS + 1, NZ - 1, 1, QUARTER), F32),
             pltpu.VMEM((ITERS, 2, 1, SIDE), F32),
@@ -514,13 +488,16 @@
             pltpu.VMEM((len(CHAINS), STEPS, CHUNKS, PIECE, FEAT), F32),
             pltpu.VMEM((len(CHAINS), STEPS, CHUNKS, PIECE, FEAT), F32),
             dma((NY + 1,)),
-            dma((2,)), dma((2,)),
-            dma, dma((NY - 1,)),
-            dma, dma((NY - 1,)),
+            dma, dma,
+            dma, dma((2,)),
+            dma, dma((2,)),
             dma((ITERS + 1,)), dma((ITERS + 1,)),
             dma((ITERS,)), dma((ITERS,)),
             dma((ITERS,)), dma((ITERS,)),
             dma((ITERS,)), dma((ITERS,)),
+            dma, dma,
+            dma, dma,
+            dma, dma,
             dma, dma,
             dma, dma,
             dma, dma,

time: 94.4 us -> 92.7 us (0.982); the launches traced: 92.5 us -> 92.5 us
  no operation moved by 1% of the time
where the time goes in v5:
time: 92.7 us; the launch traced here: 92.5 us
  Pallas kernels  90 us (97%)
  between operations  1.28 us (1%)
  local copies, waits for them, and re-layouts  1.24 us (1%)
    pallas_call x1, Pallas kernels, shards(): pl.pallas_call(kernel, out_shape=(jax.ShapeDtypeStruct((BLOCK, FEAT), F32...  90 us

profile of v5, /device:TPU:1, one launch (start us, length us, event | category | flops | bytes accessed | tf_op | source)
XLA Modules:
  0.0 92.5 jit_solution(10997573168244749670)
XLA Ops:
  1.3 90.0 %sinkhorn_assign.1 = (f32[64,256]{1,0:T(8,128)S(1)}, f32[4,1,1024]{2,1,0:T(1,128)S(1)}) custom-call(s32[1]{0:T(128)S(6)} %copy.7.counts_ref, bf16[512,256]{1,0:T(8,128)(2,1)} %lab_hbm.1, bf16[4096,256]{1,0:T(8,128)(2,1)} %cen_hbm.1), custom_call_target="tpu_custom_call" | custom-call | tf_op jit(solution)/shard_map/sinkhorn_assign/pallas_call | solution.py:448
  91.3 0.6 copy.8
  91.9 0.6 copy.9

commit v6 on v5

--- a/solution.py
+++ b/solution.py
@@ -31,6 +31,7 @@
 CHAINS = ((8, 1, 4), (7, -1, 4), (4, 1, 4), (3, -1, 3))
 STEPS = max(messages for _, _, messages in CHAINS)
 PIECE = BLOCK // CHUNKS
+QUAD = 4
 SHARE = HALF // NX
 
 
@@ -103,6 +104,9 @@
     xy_land,
     half_src,
     half_land,
+    quad_land,
+    ring_src,
+    ring_land,
     mass_src,
     mass_land,
     stat_src,
@@ -115,6 +119,8 @@
     s_core, r_core,
     s_xy, r_xy,
     s_half, r_half,
+    s_quad, r_quad,
+    s_ring, r_ring,
     s_mass, r_mass,
     s_far, r_far,
     s_far_x, r_far_x,
@@ -358,12 +364,12 @@
         z_src[turn] = joined(
             lax.dot_general(scale_rows, gibbs_t[...], NT, preferred_element_type=F32)
         )
-        z_send(turn)
 
     col_scale = 1.0 / z_total(0)
     for turn in range(ITERS):
         if turn:
             col_stage(turn)
+            z_send(turn)
             col_scale = 1.0 / z_total(turn)
         row_stage(turn, col_scale)
 
@@ -406,16 +412,26 @@
 
     stat_step(0)
     col_stage(ITERS)
-    last_sends = pending.pop()
+    for d in range(1, QUAD):
+        near = z // QUAD * QUAD + lax.rem(z + d, QUAD)
+        send(z_src.at[ITERS], quad_land.at[d - 1], s_quad, r_quad, (y * NZ + near, cent))
     for wait in pending:
         wait()
-    pending[:] = [last_sends]
-    for step in range(1, STEPS):
+    pending.clear()
+    sent_later(quad_land, s_quad, r_quad)
+    stat_step(1)
+    arrived(quad_land, s_quad, r_quad)
+    ring_src[...] = z_src[ITERS] + quad_land[0] + quad_land[1] + quad_land[2]
+    for d in (2, 1, 3):
+        send(ring_src, ring_land.at[d - 1], s_ring, r_ring, at(dz=d * QUAD))
+    sent_later(ring_land, s_ring, r_ring)
+    for step in range(2, STEPS):
         own = stat_step(step)
     for chain, (_, _, messages) in enumerate(CHAINS):
         sent_later(stat_src.at[chain, 0:messages], s_stat.at[chain], r_stat.at[chain, 0, 0])
 
-    mass = col_scale * z_total(ITERS)
+    arrived(ring_land, s_ring, r_ring)
+    mass = col_scale * (ring_src[...] + ring_land[0] + ring_land[1] + ring_land[2])
     mass_src[...] = mass
     for dy in Y_OFFSETS:
         send(mass_src, mass_land.at[dy - 1], s_mass, r_mass, at(dy=dy))
@@ -476,13 +492,16 @@
             pltpu.VMEM((NX, SHARE, FEAT), F32),
             pltpu.VMEM((2, EXTRA, FEAT), F32),
             pltpu.VMEM((ITERS + 1, 1, QUARTER), F32),
-            pltpu.VMEM((ITERS + 1, NZ - 1, 1, QUARTER), F32),
+            pltpu.VMEM((ITERS, NZ - 1, 1, QUARTER), F32),
             pltpu.VMEM((ITERS, 2, 1, SIDE), F32),
             pltpu.VMEM((ITERS, 1, SIDE), F32),
             pltpu.VMEM((ITERS, 1, SIDE), F32),
             pltpu.VMEM((ITERS, NY * NX - 1, 1, SIDE), F32),
             pltpu.VMEM((ITERS, 1, SIDE), F32),
             pltpu.VMEM((ITERS, 1, SIDE), F32),
+            pltpu.VMEM((QUAD - 1, 1, QUARTER), F32),
+            pltpu.VMEM((1, QUARTER), F32),
+            pltpu.VMEM((NZ // QUAD - 1, 1, QUARTER), F32),
             pltpu.VMEM((1, QUARTER), F32),
             pltpu.VMEM((NY - 1, 1, QUARTER), F32),
             pltpu.VMEM((len(CHAINS), STEPS, CHUNKS, PIECE, FEAT), F32),
@@ -491,10 +510,12 @@
             dma, dma,
             dma, dma((2,)),
             dma, dma((2,)),
-            dma((ITERS + 1,)), dma((ITERS + 1,)),
             dma((ITERS,)), dma((ITERS,)),
             dma((ITERS,)), dma((ITERS,)),
             dma((ITERS,)), dma((ITERS,)),
+            dma((ITERS,)), dma((ITERS,)),
+            dma, dma,
+            dma, dma,
             dma, dma,
             dma, dma,
             dma, dma,

time: 92.7 us -> 91.3 us (0.985)
  Pallas kernels: 90 us -> 88.6 us
    pallas_call x1, Pallas kernels: 90 us -> 88.6 us  [shards(): pl.pallas_call(kernel, out_shape=(jax.ShapeDtypeStruct((BLOCK, FEAT), F32...]
where the time goes in v6:
time: 91.3 us; the launch traced here: 91.2 us
  Pallas kernels  88.6 us (97%)
  between operations  1.28 us (1%)
  local copies, waits for them, and re-layouts  1.24 us (1%)
    pallas_call x1, Pallas kernels, shards(): pl.pallas_call(kernel, out_shape=(jax.ShapeDtypeStruct((BLOCK, FEAT), F32...  88.6 us

profile of v6, /device:TPU:1, one launch (start us, length us, event | category | flops | bytes accessed | tf_op | source)
XLA Modules:
  0.0 91.2 jit_solution(11487712424195800085)
XLA Ops:
  1.3 88.6 %sinkhorn_assign.1 = (f32[64,256]{1,0:T(8,128)S(1)}, f32[4,1,1024]{2,1,0:T(1,128)S(1)}) custom-call(s32[1]{0:T(128)S(6)} %copy.7.counts_ref, bf16[512,256]{1,0:T(8,128)(2,1)} %lab_hbm.1, bf16[4096,256]{1,0:T(8,128)(2,1)} %cen_hbm.1), custom_call_target="tpu_custom_call" | custom-call | tf_op jit(solution)/shard_map/sinkhorn_assign/pallas_call | solution.py:464
  89.9 0.6 copy.8
  90.6 0.6 copy.9

commit v7 on v6

--- a/solution.py
+++ b/solution.py
@@ -356,22 +356,29 @@
         send(half_src.at[turn], half_land.at[turn], s_half.at[turn], r_half.at[turn], partner)
         sent_later(half_land.at[turn], s_half.at[turn], r_half.at[turn])
         row_scale[:, mine] = scale
+        mine_sums = col_sums(scale, k)
         arrived(half_land.at[turn], s_half.at[turn], r_half.at[turn])
         row_scale[:, pl.ds(pl.multiple_of(other * SIDE, SIDE), SIDE)] = half_land[turn]
-
-    def col_stage(turn):
-        scale_rows = split_rows(row_scale[...])
-        z_src[turn] = joined(
-            lax.dot_general(scale_rows, gibbs_t[...], NT, preferred_element_type=F32)
-        )
+        return mine_sums
+
+    def col_sums(scale, half):
+        columns = pl.ds(pl.multiple_of(half * SIDE, SIDE), SIDE)
+        return joined(
+            lax.dot_general(
+                split_rows(scale), gibbs_t[:, columns], NT, preferred_element_type=F32
+            )
+        )
+
+    def col_stage(turn, mine_sums):
+        z_src[turn] = mine_sums + col_sums(half_land[turn - 1], other)
 
     col_scale = 1.0 / z_total(0)
     for turn in range(ITERS):
         if turn:
-            col_stage(turn)
+            col_stage(turn, mine_sums)
             z_send(turn)
             col_scale = 1.0 / z_total(turn)
-        row_stage(turn, col_scale)
+        mine_sums = row_stage(turn, col_scale)
 
     def block_stats(offsets, piece):
         for slot, offset in enumerate(offsets):
@@ -411,7 +418,7 @@
         return rest
 
     stat_step(0)
-    col_stage(ITERS)
+    col_stage(ITERS, mine_sums)
     for d in range(1, QUAD):
         near = z // QUAD * QUAD + lax.rem(z + d, QUAD)
         send(z_src.at[ITERS], quad_land.at[d - 1], s_quad, r_quad, (y * NZ + near, cent))

time: 91.3 us -> 90.5 us (level)
  Pallas kernels: 88.6 us -> 87.6 us
    pallas_call x1, Pallas kernels: 88.6 us -> 87.6 us  [shards(): pl.pallas_call(kernel, out_shape=(jax.ShapeDtypeStruct((BLOCK, FEAT), F32...]
where the time goes in v7:
time: 90.5 us; the launch traced here: 90.1 us
  Pallas kernels  87.6 us (97%)
  between operations  1.28 us (1%)
  local copies, waits for them, and re-layouts  1.24 us (1%)
    pallas_call x1, Pallas kernels, shards(): pl.pallas_call(kernel, out_shape=(jax.ShapeDtypeStruct((BLOCK, FEAT), F32...  87.6 us

profile of v7, /device:TPU:1, one launch (start us, length us, event | category | flops | bytes accessed | tf_op | source)
XLA Modules:
  0.0 90.1 jit_solution(4654054644251456972)
XLA Ops:
  1.3 87.6 %sinkhorn_assign.1 = (f32[64,256]{1,0:T(8,128)S(1)}, f32[4,1,1024]{2,1,0:T(1,128)S(1)}) custom-call(s32[1]{0:T(128)S(6)} %copy.7.counts_ref, bf16[512,256]{1,0:T(8,128)(2,1)} %lab_hbm.1, bf16[4096,256]{1,0:T(8,128)(2,1)} %cen_hbm.1), custom_call_target="tpu_custom_call" | custom-call | tf_op jit(solution)/shard_map/sinkhorn_assign/pallas_call | solution.py:471
  88.8 0.6 copy.8
  89.5 0.6 copy.9
